TPU v7x, 32 devices: a whole 2x2x4 slice. The times are simulated.
32 devices in a mesh: groups: 2 (over x), tensor: 4 (over y, core), dp: 4 (over z).
Axes of the slice: x: 2, y: 2, z: 4, core: 2. Of those that a mesh axis runs over, the one named last changes fastest.
Arguments:
- layer_inputs: bfloat16 [2, 16, 512, 28672], P(None, ('groups', 'dp'), None, 'tensor'), parts along dimension 1, may hold values from -6 to 6
- output_grads: bfloat16 [2, 16, 512, 8192], P(None, ('groups', 'dp'), None, 'tensor'), parts along dimension 1, may hold values from -6 to 6
- in_proj: bfloat16 [2, 28672, 32], P(None, 'tensor'), may hold values from -0.03125 to 0.03125
- out_proj: bfloat16 [2, 8192, 32], P(None, 'tensor'), may hold values from -0.0625 to 0.0625
- valid_counts: int32 [16], P(('groups', 'dp')), parts along dimension 0, may hold values from 128 to 512
- assignment: int32 [16], P('groups'), parts along dimension 0, may hold values from 0 to 7, each once
Outputs:
- seq_grads: float32 [16, 2048], P(('groups', 'dp'), 'tensor'), parts along dimension 0
- fisher: float32 [4096, 2048], P(('groups', 'dp'), 'tensor'), parts along dimension 0
There are 2 independent parts, one for each index of `groups`. A program takes and returns all parts, laid end to end along the dimension named above; an argument that names none is the same for every part. Nothing has to cross between parts.
All inputs are finite; a program needn't handle non-finite values.
Results may differ from a plain program's by a relative error of at most 0.0003.
Values sent between devices are 32-bit elements; how exact they have to be, the bound alone decides.
No kernel may reach another device: no remote copies, remote signals or barrier semaphores. Data moves between devices by JAX's collectives and lax.ppermute only.
A program may use at most 128 MiB of HBM per device.

v0:
```python
import jax
import jax.numpy as jnp
from jax import lax
from jax.sharding import PartitionSpec as P


def project_rows(layer_inputs, output_grads, in_proj, out_proj, valid_counts, count):
    position = jnp.arange(count, dtype=jnp.int32)
    keep = (position[:, None] < valid_counts[None, :]).astype(jnp.float32)
    pieces = []
    for layer in range(layer_inputs.shape[0]):
        outer = jnp.einsum(
            "std,dr->tsr", output_grads[layer], out_proj[layer], preferred_element_type=jnp.float32
        )
        inner = jnp.einsum(
            "stf,fr->tsr", layer_inputs[layer], in_proj[layer], preferred_element_type=jnp.float32
        )
        pieces.append(outer)
        pieces.append(inner * keep[:, :, None])
    return jnp.concatenate(pieces, axis=2)


def sequence_grads(term, layers, rank):
    split = term.reshape(term.shape[0], term.shape[1], layers, 2, rank)
    product = jnp.einsum(
        "tsli,tslj->slij", split[:, :, :, 0], split[:, :, :, 1], precision=lax.Precision.HIGHEST
    )
    return product.reshape(term.shape[1], layers * rank * rank)


def on_device(layer_inputs, output_grads, in_proj, out_proj, valid_counts, assignment):
    layers = layer_inputs.shape[0]
    rank = in_proj.shape[2]
    seq_len = layer_inputs.shape[2]
    term = project_rows(layer_inputs, output_grads, in_proj, out_proj, valid_counts, seq_len)
    summed = lax.psum(term, "tensor")
    vectors = sequence_grads(summed, layers, rank)
    vectors = vectors * seq_len ** (-0.5)
    gathered = lax.all_gather(vectors, "dp", axis=0, tiled=True)
    total_seqs = gathered.shape[0]
    feat = gathered.shape[1]
    row_width = feat // lax.axis_size("dp")
    col_width = feat // lax.axis_size("tensor")
    dp_index = lax.axis_index("dp")
    tensor_index = lax.axis_index("tensor")
    columns = lax.dynamic_slice_in_dim(gathered, tensor_index * col_width, col_width, 1)
    row_block = lax.dynamic_slice_in_dim(gathered, dp_index * row_width, row_width, 1)
    fisher = (
        lax.dot_general(
            row_block, columns, (((0,), (0,)), ((), ())), precision=lax.Precision.HIGHEST
        )
        / total_seqs
    )
    local_seqs = vectors.shape[0]
    owners = dp_index * local_seqs + jnp.arange(local_seqs, dtype=jnp.int32)
    selector = (assignment[None, :] == owners[:, None]).astype(jnp.float32)
    seq_grads = jnp.dot(selector, columns, precision=lax.Precision.HIGHEST)
    return (seq_grads, fisher)


def solution(mesh):
    return jax.shard_map(
        on_device,
        mesh=mesh,
        in_specs=(
            P(None, ("groups", "dp"), None, "tensor"),
            P(None, ("groups", "dp"), None, "tensor"),
            P(None, "tensor", None),
            P(None, "tensor", None),
            P(("groups", "dp")),
            P("groups"),
        ),
        out_specs=(P(("groups", "dp"), "tensor"), P(("groups", "dp"), "tensor")),
        check_vma=False,
    )
```

profile of v0, /device:TPU:0, one launch (start us, length us, event | category | flops | bytes accessed | tf_op | source)
XLA Modules:
  0.0 87.9 jit_solution(14891858318943291272)
XLA Ops:
  7.2 0.0 copy-start
  7.2 0.0 all-reduce.2.cloned.1.call-start
  7.2 0.8 compare_convert_fusion
  8.0 0.0 slice-start
  8.0 0.0 copy-start.1
  8.0 7.9 %fusion.24 = f32[512,2,32]{0,2,1:T(8,128)S(1)} fusion(bf16[2,2,512,7168]{3,2,1,0:T(8,128)(2,1)} %param.6, bf16[2,7168,32]{1,2,0:T(8,128)(2,1)} %param.8, f32[512,2]{0,1:T(2,128)S(1)} %compare_convert_fusion), kind=kOutput, calls=%fused_computation.17 | convolution fusion | flops 469794816 | bytes 15273984 | tf_op jit(solution)/shard_map/stf,fr->tsr/dot_general | solution.py:15
  15.9 0.0 copy-done
  15.9 0.0 slice-start.1
  15.9 0.0 copy-start.2
  15.9 7.8 %fusion.27 = f32[512,2,32]{0,2,1:T(8,128)S(1)} fusion(bf16[2,2,512,7168]{3,2,1,0:T(8,128)(2,1)} %param.6, bf16[2,7168,32]{1,2,0:T(8,128)(2,1)S(1)} %copy-done, f32[512,2]{0,1:T(2,128)S(1)} %compare_convert_fusion), kind=kOutput, calls=%fused_computation.18 | convolution fusion | flops 469794816 | bytes 15273984 | tf_op jit(solution)/shard_map/stf,fr->tsr/dot_general | solution.py:15
  23.8 0.0 slice-done
  23.8 0.0 copy-done.1
  23.8 0.0 slice-done.1
  23.8 1.3 %fusion.15 = f32[512,2,32]{0,2,1:T(8,128)S(1)} fusion(bf16[2,2,512,2048]{3,2,1,0:T(8,128)(2,1)S(1)} %bitcast.63, bf16[2,2048,32]{1,2,0:T(8,128)(2,1)S(1)} %copy-done.1), kind=kOutput, calls=%fused_computation.14 | convolution fusion | flops 134217728 | bytes 4456448 | tf_op jit(solution)/shard_map/std,dr->tsr/dot_general | solution.py:12
  25.2 1.3 %fusion.12 = f32[512,2,32]{0,2,1:T(8,128)S(1)} fusion(bf16[2,2,512,2048]{3,2,1,0:T(8,128)(2,1)S(1)} %bitcast.63, bf16[2,2048,32]{1,2,0:T(8,128)(2,1)S(1)} %copy-done.1), kind=kOutput, calls=%fused_computation.13 | convolution fusion | flops 134217728 | bytes 4456448 | tf_op jit(solution)/shard_map/std,dr->tsr/dot_general | solution.py:12
  26.6 0.8 copy.9
  27.4 0.0 all-reduce.2.cloned.1.call-update
  27.4 36.0 %all-reduce.2.cloned.1.call-done = f32[512,2,2,2,32]{0,4,2,1,3:T(8,128)} async-done(((f32[512,2,2,2,32]{0,4,2,1,3:T(8,128)}), f32[512,2,2,2,32]{0,4,2,1,3:T(8,128)}) %all-reduce.2.cloned.1.call-update) | async-done | bytes 524304 | tf_op jit(solution)/shard_map/psum | solution.py:36
  63.5 1.4 %convolution_multiply_fusion.1 = f32[2,2,32,32]{3,2,1,0:T(8,128)S(1)} fusion(f32[512,2,2,2,32]{0,4,2,1,3:T(8,128)} %all-reduce.2.cloned.1.call-done), kind=kOutput, calls=%fused_computation.19 | convolution fusion | flops 25169920 | bytes 540672 | tf_op jit(solution)/shard_map/tsli,tslj->slij/dot_general | solution.py:25
  64.9 0.1 reshape.35
  65.0 13.2 %all-gather = f32[4,2,2048]{2,1,0:T(2,128)S(1)} all-gather(f32[1,2,2048]{2,1,0:T(2,128)S(1)} %reshape.35), channel_id=1, replica_groups=mesh['groups'=2,'tensor'=4,'dp'=4] {'dp'}, dimensions={0}, use_global_device_ids=true | all-gather | bytes 81920 | tf_op jit(solution)/shard_map/all_gather | solution.py:39
  78.3 2.0 %convolution_multiply_fusion = f32[512,512]{1,0:T(8,128)} fusion(f32[8,2048]{1,0:T(8,128)S(1)} %reshape.36, s32[]{:T(128)S(6)} %select_n.7, s32[]{:T(128)S(6)} %select_n.6), kind=kOutput, calls=%fused_computation.12 | convolution fusion | flops 25427968 | bytes 1081352 | tf_op jit(solution)/shard_map/dot_general | solution.py:49
  80.3 0.0 copy-done.2
  80.3 0.8 fusion.40
  (4 shorter events, 0.1 us)
Async XLA Ops:
  7.2 8.7 %copy-start = (bf16[2,7168,32]{1,2,0:T(8,128)(2,1)S(1)}, bf16[2,7168,32]{1,2,0:T(8,128)(2,1)}, u32[]{:S(2)}) copy-start(bf16[2,7168,32]{1,2,0:T(8,128)(2,1)} %param.8) | copy-start | bytes 2752516
  7.2 56.3 %all-reduce.2.cloned.1.call-start = ((), (), s32[]{:S(2)}) async-start(), calls=%async_computation | async-start | bytes 1048576 | tf_op jit(solution)/shard_map/psum | solution.py:36
  8.0 15.8 %slice-start = ((s8[8388608]{0:T(1024)(128)(4,1)}), s8[4194304]{0:T(1024)(128)(4,1)S(1)}, s32[]{:S(2)}) async-start(s8[8388608]{0:T(1024)(128)(4,1)} %bitcast.62), calls=%async_computation.1 | async-start | bytes 8388608
  8.0 15.8 %copy-start.1 = (bf16[2,2048,32]{1,2,0:T(8,128)(2,1)S(1)}, bf16[2,2048,32]{1,2,0:T(8,128)(2,1)}, u32[]{:S(2)}) copy-start(bf16[2,2048,32]{1,2,0:T(8,128)(2,1)} %param.9) | copy-start | bytes 786436
  15.9 7.9 %slice-start.1 = ((s8[8388608]{0:T(1024)(128)(4,1)}), s8[4194304]{0:T(1024)(128)(4,1)S(1)}, s32[]{:S(2)}) async-start(s8[8388608]{0:T(1024)(128)(4,1)} %bitcast.62), calls=%async_computation.2 | async-start | bytes 8388608
  15.9 64.4 %copy-start.2 = (s32[8]{0:T(128)S(1)}, s32[8]{0:T(128)}, u32[]{:S(2)}) copy-start(s32[8]{0:T(128)} %param.11) | copy-start | bytes 100
Sparse Core Ops, SparseCore 0:
  27.5 35.8 all-reduce.1
where the time goes:
time: 88.1 us; the launch traced here: 87.9 us
  waiting for transfers between devices  36.1 us (41%)
  matrix products  22.6 us (26%)
  between operations  14.1 us (16%)
  blocking collectives  13.2 us (15%)
  local copies, waits for them, and re-layouts  1.01 us (1%)
    psum x1, waiting for transfers between devices, on_device(): summed = lax.psum(term, 'tensor')  36 us
    dot_general x2, matrix products, project_rows(): jnp.einsum('stf,fr->tsr', layer_inputs[layer], in_proj[layer], preferred_...  15.7 us
    all_gather x1, blocking collectives, on_device(): gathered = lax.all_gather(vectors, 'dp', axis=0, tiled=True)  13.2 us
    dot_general x2, matrix products, project_rows(): jnp.einsum('std,dr->tsr', output_grads[layer], out_proj[layer], preferred...  2.67 us
    dot_general x1, matrix products, on_device(): lax.dot_general(row_block, columns, (((0,), (0,)), ((), ())), precision=l...  2.01 us
  transfers between devices with their start and end apart: 1, of which 1 were waited for; matrix products, arithmetic and copies ran while one was open for 0% of the time, Pallas kernels for 0%

commit v1 on v0

v1 whole, which is shorter than its diff:
```python
import functools

import jax
import jax.numpy as jnp
from jax import lax
from jax.experimental import pallas as pl
from jax.experimental.pallas import tpu as pltpu
from jax.sharding import PartitionSpec as P

NT = (((1,), (1,)), ((), ()))
TN = (((0,), (0,)), ((), ()))


def pieces(value):
    high = value.astype(jnp.bfloat16)
    low = (value - high.astype(jnp.float32)).astype(jnp.bfloat16)
    return high, low


def project_kernel(step, width_x, width_g, depth, counts, x, g, wi, wo, send, keep, xb, gb, wib, wob, sems, wsems):
    layers, rank = wi.shape[0], wi.shape[1]
    tokens = x.shape[2]
    blocks = tokens // step
    core = lax.rem(lax.axis_index("tensor"), 2)
    slots = (1 - core, core)
    valid = [counts[s] for s in slots]
    used = [jnp.clip((v + (step - 1)) // step, 1, blocks) for v in valid]
    jobs = []
    for j in range(2):
        for l in range(layers):
            for k in range(0, x.shape[3], width_x):
                jobs.append((0, j, l, k, width_x))
            for k in range(0, g.shape[3], width_g):
                jobs.append((1, j, l, k, width_g))

    def copy(i, v):
        which, j, l, k, width = jobs[i]
        src, dst = ((x, xb), (g, gb))[which]
        rows, cols = pl.ds(0, step * v), pl.ds(k, width)
        return pltpu.make_async_copy(src.at[l, slots[j], rows, cols], dst.at[l, j, rows, cols], sems.at[i])

    def start(i):
        if i < len(jobs):
            for v in range(1, blocks + 1):

                @pl.when(used[jobs[i][1]] == v)
                def _():
                    copy(i, v).start()

    weights = [pltpu.make_async_copy(wi, wib, wsems.at[0]), pltpu.make_async_copy(wo, wob, wsems.at[1])]
    for c in weights:
        c.start()
    for i in range(depth):
        start(i)
    send[...] = jnp.zeros_like(send)
    keep[...] = jnp.zeros_like(keep)
    for c in weights:
        c.wait()
    for i, (which, j, l, k, width) in enumerate(jobs):
        start(i + depth)
        data, weight = ((xb, wib), (gb, wob))[which]
        out = (send, keep)[j]
        first = (rank, 0)[which]
        last = k + width == data.shape[3]
        for v in range(1, blocks + 1):

            @pl.when(used[j] == v)
            def _():
                copy(i, v).wait()
                n = step * v
                d = lax.dot_general(
                    weight[l, :, k : k + width], data[l, j, 0:n, k : k + width], NT, preferred_element_type=jnp.float32
                )
                if k > 0:
                    d = d + out[l, first : first + rank, 0:n]
                if which == 0 and last:
                    d = jnp.where(lax.broadcasted_iota(jnp.int32, (rank, n), 1) < valid[j], d, 0.0)
                out[l, first : first + rank, 0:n] = d


def project(layer_inputs, output_grads, in_proj, out_proj, valid_counts):
    layers, seqs, tokens, ff = layer_inputs.shape
    d = output_grads.shape[3]
    rank = in_proj.shape[2]
    width_x, width_g = ff // 4, d
    jobs = 2 * layers * (ff // width_x + d // width_g)
    anywhere = pl.BlockSpec(memory_space=pl.ANY)
    out = jax.ShapeDtypeStruct((layers, 2 * rank, tokens), jnp.float32)
    return pl.pallas_call(
        functools.partial(project_kernel, tokens // 4, width_x, width_g, 3),
        out_shape=(out, out),
        in_specs=[pl.BlockSpec(memory_space=pltpu.SMEM)] + [anywhere] * 4,
        out_specs=(pl.BlockSpec(memory_space=pltpu.VMEM),) * 2,
        scratch_shapes=[
            pltpu.VMEM((layers, seqs, tokens, ff), jnp.bfloat16),
            pltpu.VMEM((layers, seqs, tokens, d), jnp.bfloat16),
            pltpu.VMEM((layers, rank, ff), jnp.bfloat16),
            pltpu.VMEM((layers, rank, d), jnp.bfloat16),
            pltpu.SemaphoreType.DMA((jobs,)),
            pltpu.SemaphoreType.DMA((2,)),
        ],
        compiler_params=pltpu.CompilerParams(vmem_limit_bytes=48 * 2**20),
        name="project",
    )(valid_counts, layer_inputs, output_grads, jnp.swapaxes(in_proj, 1, 2), jnp.swapaxes(out_proj, 1, 2))


def product_kernel(scale, own, received, out, square):
    layers, rank = own.shape[0], own.shape[1] // 2
    per_row = 128 // rank
    rows = rank // per_row
    for l in range(layers):
        outer_high, outer_low = pieces(own[l, 0:rank] + received[l, 0:rank])
        inner_high, inner_low = pieces(own[l, rank:] + received[l, rank:])
        both = lax.dot_general(
            jnp.concatenate([outer_high, outer_low], axis=0), inner_high, NT, preferred_element_type=jnp.float32
        )
        third = lax.dot_general(outer_high, inner_low, NT, preferred_element_type=jnp.float32)
        square[l] = (both[0:rank] + (both[rank:] + third)) * scale
        out[l * rows : (l + 1) * rows, :] = jnp.concatenate(
            [square[l, pl.ds(r, rows, stride=per_row), :] for r in range(per_row)], axis=1
        )


def product(own, received):
    layers, double, tokens = own.shape
    rank = double // 2
    return pl.pallas_call(
        functools.partial(product_kernel, tokens ** (-0.5)),
        out_shape=jax.ShapeDtypeStruct((layers * rank * rank // 128, 128), jnp.float32),
        in_specs=[pl.BlockSpec(memory_space=pltpu.VMEM)] * 2,
        out_specs=pl.BlockSpec(memory_space=pltpu.VMEM),
        scratch_shapes=[pltpu.VMEM((layers, rank, rank), jnp.float32)],
        name="product",
    )(own, received)


def gram_kernel(assignment, vectors, seq_grads, fisher):
    total = vectors.shape[0]
    local = seq_grads.shape[0]
    tensor, dp = lax.axis_index("tensor"), lax.axis_index("dp")
    core = lax.rem(tensor, 2)
    row_lanes, col_lanes = fisher.shape[0] // 128, fisher.shape[1] // 128
    rows = jnp.concatenate([vectors[:, dp * row_lanes + r, :] for r in range(row_lanes)], axis=1)
    cols = jnp.concatenate([vectors[:, tensor * col_lanes + r, :] for r in range(col_lanes)], axis=1)
    rows_high, rows_low = pieces(rows)
    cols_high, cols_low = pieces(cols)
    fisher[...] = lax.dot_general(
        jnp.concatenate([rows_high, rows_high, rows_low], axis=0),
        jnp.concatenate([cols_high, cols_low, cols_high], axis=0),
        TN,
        preferred_element_type=jnp.float32,
    ) * (1.0 / total)
    for r in range(local):
        chosen = jnp.zeros((1, cols.shape[1]), jnp.float32)
        for place in range(total):
            slot = lax.bitwise_xor(dp, place % (total // 2)) * 2 + lax.bitwise_xor(core, place // (total // 2))
            chosen = jnp.where(assignment[slot] == dp * local + r, cols[place : place + 1, :], chosen)
        seq_grads[r : r + 1, :] = chosen


def gram(vectors, assignment, local, row_width, col_width):
    return pl.pallas_call(
        gram_kernel,
        out_shape=(
            jax.ShapeDtypeStruct((local, col_width), jnp.float32),
            jax.ShapeDtypeStruct((row_width, col_width), jnp.float32),
        ),
        in_specs=[pl.BlockSpec(memory_space=pltpu.SMEM), pl.BlockSpec(memory_space=pltpu.VMEM)],
        out_specs=(pl.BlockSpec(memory_space=pltpu.VMEM),) * 2,
        name="gram",
    )(assignment, vectors)


def swap(value, axis, bit):
    size = lax.axis_size(axis)
    return lax.ppermute(value, axis, [(i, i ^ bit) for i in range(size)])


def two_level(layer_inputs, output_grads, in_proj, out_proj, valid_counts, assignment):
    layers, local = layer_inputs.shape[:2]
    rank = in_proj.shape[2]
    feat = layers * rank * rank
    send, keep = project(layer_inputs, output_grads, in_proj, out_proj, valid_counts)
    chip = keep + swap(send, "tensor", 1)
    vector = product(chip, swap(chip, "tensor", 2))
    gathered = vector[None]
    for bit in (1, 2):
        gathered = jnp.concatenate([gathered, swap(gathered, "dp", bit)], axis=0)
    gathered = jnp.concatenate([gathered, swap(gathered, "tensor", 1)], axis=0)
    return gram(gathered, assignment, local, feat // lax.axis_size("dp"), feat // lax.axis_size("tensor"))


def any_sizes(layer_inputs, output_grads, in_proj, out_proj, valid_counts, assignment):
    layers, local, tokens = layer_inputs.shape[:3]
    rank = in_proj.shape[2]
    position = jnp.arange(tokens, dtype=jnp.int32)
    keep = (position[None, :] < valid_counts[:, None]).astype(jnp.float32)
    outer = jnp.einsum("lstd,ldr->lsrt", output_grads, out_proj, preferred_element_type=jnp.float32)
    inner = jnp.einsum("lstf,lfr->lsrt", layer_inputs, in_proj, preferred_element_type=jnp.float32)
    summed = lax.psum(jnp.concatenate([outer, inner * keep[None, :, None, :]], axis=2), "tensor")
    product = jnp.einsum(
        "lsit,lsjt->slij", summed[:, :, :rank], summed[:, :, rank:], precision=lax.Precision.HIGHEST
    )
    vectors = product.reshape(local, layers * rank * rank) * tokens ** (-0.5)
    gathered = lax.all_gather(vectors, "dp", axis=0, tiled=True)
    total, feat = gathered.shape
    dp_index, tensor_index = lax.axis_index("dp"), lax.axis_index("tensor")
    row_width, col_width = feat // lax.axis_size("dp"), feat // lax.axis_size("tensor")
    cols = lax.dynamic_slice_in_dim(gathered, tensor_index * col_width, col_width, 1)
    rows = lax.dynamic_slice_in_dim(gathered, dp_index * row_width, row_width, 1)
    fisher = lax.dot_general(rows, cols, TN, precision=lax.Precision.HIGHEST) / total
    owners = dp_index * local + jnp.arange(local, dtype=jnp.int32)
    selector = (assignment[None, :] == owners[:, None]).astype(jnp.float32)
    return jnp.dot(selector, cols, precision=lax.Precision.HIGHEST), fisher


def on_device(*arrays):
    local = arrays[0].shape[1]
    if lax.axis_size("tensor") == 4 and lax.axis_size("dp") == 4 and local == 2:
        return two_level(*arrays)
    return any_sizes(*arrays)


def solution(mesh):
    return jax.shard_map(
        on_device,
        mesh=mesh,
        in_specs=(
            P(None, ("groups", "dp"), None, "tensor"),
            P(None, ("groups", "dp"), None, "tensor"),
            P(None, "tensor", None),
            P(None, "tensor", None),
            P(("groups", "dp")),
            P("groups"),
        ),
        out_specs=(P(("groups", "dp"), "tensor"), P(("groups", "dp"), "tensor")),
        check_vma=False,
    )
```

time: 88.1 us -> 46.8 us (0.53)
  waiting for transfers between devices: 36.1 us -> 12.5 us
  matrix products: 22.6 us -> 0 us
  Pallas kernels: 0 us -> 16.8 us
  between operations: 14.1 us -> 0.67 us
  blocking collectives: 13.2 us -> 0 us
  starting transfers between devices: 0.04 us -> 11.3 us
  local copies, waits for them, and re-layouts: 1.01 us -> 3.49 us
  other arithmetic: 0.85 us -> 2.76 us
    psum x1 -> x0, waiting for transfers between devices: 36 us -> none  [on_device(): summed = lax.psum(term, 'tensor')]
    dot_general x7 -> x0, matrix products: 22.6 us -> none  [the longest x2 15.7 us: project_rows(): jnp.einsum('stf,fr->tsr', layer_inputs[layer], in_proj[layer], preferred_...]
    pallas_call x0 -> x3, Pallas kernels: none -> 16.8 us  [the longest x1 12.7 us: project(): pl.pallas_call(functools.partial(project_kernel, tokens // 4, width_x, wi...]
    all_gather x1 -> x0, blocking collectives: 13.2 us -> none  [on_device(): gathered = lax.all_gather(vectors, 'dp', axis=0, tiled=True)]
    ppermute x0 -> x5, waiting for transfers between devices: none -> 12.5 us  [swap(): return lax.ppermute(value, axis, [(i, i ^ bit) for i in range(size)])]
    ppermute x0 -> x5, starting transfers between devices: none -> 11.3 us  [swap(): return lax.ppermute(value, axis, [(i, i ^ bit) for i in range(size)])]
    unnamed x12 -> x10, local copies, waits for them, and re-layouts: 0.17 us -> 3.49 us
    concatenate x1 -> x3, other arithmetic: 0.05 us -> 2.72 us  [the longest x2 1.4 us: two_level(): gathered = jnp.concatenate([gathered, swap(gathered, 'dp', bit)], axis=0)]
  transfers between devices with their start and end apart: 1 -> 5, of which waited for: 1 -> 5; matrix products, arithmetic and copies ran while one was open for 0% -> 0% of each run, Pallas kernels for 0% -> 0%
where the time goes in v1:
time: 46.8 us; the launch traced here: 47.5 us
  Pallas kernels  16.8 us (36%)
  waiting for transfers between devices  12.5 us (27%)
  starting transfers between devices  11.3 us (24%)
  local copies, waits for them, and re-layouts  3.49 us (7%)
  other arithmetic  2.76 us (6%)
  between operations  0.67 us (1%)
    pallas_call x1, Pallas kernels, project(): pl.pallas_call(functools.partial(project_kernel, tokens // 4, width_x, wi...  12.7 us
    ppermute x5, waiting for transfers between devices, swap(): return lax.ppermute(value, axis, [(i, i ^ bit) for i in range(size)])  12.5 us
    ppermute x5, starting transfers between devices, swap(): return lax.ppermute(value, axis, [(i, i ^ bit) for i in range(size)])  11.3 us
    unnamed x10, local copies, waits for them, and re-layouts  3.49 us
    pallas_call x1, Pallas kernels, gram(): pl.pallas_call(gram_kernel, out_shape=(jax.ShapeDtypeStruct((local, col_w...  2.15 us
    pallas_call x1, Pallas kernels, product(): pl.pallas_call(functools.partial(product_kernel, tokens ** (-0.5)), out_s...  1.9 us
    concatenate x2, other arithmetic, two_level(): gathered = jnp.concatenate([gathered, swap(gathered, 'dp', bit)], axis=0)  1.4 us
    concatenate x1, other arithmetic, two_level(): gathered = jnp.concatenate([gathered, swap(gathered, 'tensor', 1)], axis=0)  1.33 us
  transfers between devices with their start and end apart: 5, of which 5 were waited for; matrix products, arithmetic and copies ran while one was open for 0% of the time, Pallas kernels for 0%

profile of v1, /device:TPU:0, one launch (start us, length us, event | category | flops | bytes accessed | tf_op | source)
XLA Modules:
  0.0 47.5 jit_solution(3585715235416856112)
XLA Ops:
  0.6 0.0 copy-start
  0.6 1.2 %copy-done = bf16[2,7168,32]{1,2,0:T(8,128)(2,1)S(1)} copy-done((bf16[2,7168,32]{1,2,0:T(8,128)(2,1)S(1)}, bf16[2,7168,32]{1,2,0:T(8,128)(2,1)}, u32[]{:S(2)}) %copy-start) | copy-done | bytes 917528
  1.8 0.0 copy-start.1
  1.8 0.9 %copy-done.1 = bf16[2,2048,32]{1,2,0:T(8,128)(2,1)S(1)} copy-done((bf16[2,2048,32]{1,2,0:T(8,128)(2,1)S(1)}, bf16[2,2048,32]{1,2,0:T(8,128)(2,1)}, u32[]{:S(2)}) %copy-start.1) | copy-done | bytes 262168
  2.8 0.0 copy-start.2
  2.8 0.7 %copy-done.2 = s32[2]{0:T(128)S(1)} copy-done((s32[2]{0:T(128)S(1)}, s32[2]{0:T(128)}, u32[]{:S(2)}) %copy-start.2) | copy-done | bytes 32
  3.4 12.7 %project.1 = (f32[2,64,512]{2,1,0:T(8,128)S(1)}, f32[2,64,512]{2,1,0:T(8,128)S(1)}) custom-call(s32[2]{0:T(128)S(1)} %copy-done.2, bf16[2,2,512,7168]{3,2,1,0:T(8,128)(2,1)} %x.1, bf16[2,2,512,2048]{3,2,1,0:T(8,128)(2,1)} %g.1, bf16[2,32,7168]{2,1,0:T(8,128)(2,1)S(1)} %bitcast.3, bf16[2,32,2048]{2,1,0:T(8,128)(2,1)S(1)} %bitcast.4), custom_call_target="tpu_custom_call" | custom-call | tf_op jit(solution)/shard_map/project/pallas_call | solution.py:89
  16.1 0.5 collective-permute-start
  16.6 1.2 %collective-permute-done = f32[2,64,512]{2,1,0:T(8,128)S(1)} collective-permute-done((f32[2,64,512]{2,1,0:T(8,128)S(1)}, f32[2,64,512]{2,1,0:T(8,128)S(1)}, u32[]{:S(2)}, u32[]{:S(2)}) %collective-permute-start) | collective-permute-done | bytes 262176 | tf_op jit(solution)/shard_map/ppermute | solution.py:176
  17.8 0.0 copy-start.3
  17.8 3.0 %collective-permute-start.1 = (f32[2,64,512]{2,1,0:T(8,128)S(1)}, f32[2,64,512]{2,1,0:T(8,128)S(1)}, u32[]{:S(2)}, u32[]{:S(2)}) collective-permute-start(f32[2,64,512]{2,1,0:T(8,128)S(1)} %add.3.own), channel_id=1, source_target_pairs={{0,8},{4,12},{8,0},{12,4},{1,9},{5,13},{9,1},{13,5},{2,10},{6,14},... | collective-permute-start | bytes 786440 | tf_op jit(solution)/shard_map/ppermute | solution.py:176
  20.8 6.6 %collective-permute-done.1.received = f32[2,64,512]{2,1,0:T(8,128)S(1)} collective-permute-done((f32[2,64,512]{2,1,0:T(8,128)S(1)}, f32[2,64,512]{2,1,0:T(8,128)S(1)}, u32[]{:S(2)}, u32[]{:S(2)}) %collective-permute-start.1) | collective-permute-done | bytes 262176 | tf_op jit(solution)/shard_map/ppermute | solution.py:176
  27.4 0.0 copy-done.3
  27.4 0.0 copy-start.4
  27.4 0.7 %copy-done.4 = f32[2,64,512]{2,1,0:T(8,128)} copy-done((f32[2,64,512]{2,1,0:T(8,128)}, f32[2,64,512]{2,1,0:T(8,128)S(1)}, u32[]{:S(2)}) %copy-start.4) | copy-done | bytes 262168
  28.1 1.9 %product.1 = f32[16,128]{1,0:T(8,128)} custom-call(f32[2,64,512]{2,1,0:T(8,128)} %copy-done.3, f32[2,64,512]{2,1,0:T(8,128)} %copy-done.4), custom_call_target="tpu_custom_call" | custom-call | tf_op jit(solution)/shard_map/product/pallas_call | solution.py:127
  30.0 3.8 %collective-permute-start.2 = (f32[1,16,128]{2,1,0:T(8,128)}, f32[1,16,128]{2,1,0:T(8,128)S(1)}, u32[]{:S(2)}, u32[]{:S(2)}) collective-permute-start(f32[1,16,128]{2,1,0:T(8,128)} %bitcast.5), channel_id=1, source_target_pairs={{0,1},{1,0},{2,3},{3,2},{4,5},{5,4},{6,7},{7,6},{8,9},{9,8},{10,11... | collective-permute-start | bytes 24584 | tf_op jit(solution)/shard_map/ppermute | solution.py:176
  33.9 1.8 %collective-permute-done.2 = f32[1,16,128]{2,1,0:T(8,128)S(1)} collective-permute-done((f32[1,16,128]{2,1,0:T(8,128)}, f32[1,16,128]{2,1,0:T(8,128)S(1)}, u32[]{:S(2)}, u32[]{:S(2)}) %collective-permute-start.2) | collective-permute-done | bytes 8224 | tf_op jit(solution)/shard_map/ppermute | solution.py:176
  35.7 0.7 %pad_maximum_fusion.2 = f32[2,16,128]{2,1,0:T(8,128)S(1)} fusion(f32[1,16,128]{2,1,0:T(8,128)S(1)} %collective-permute-done.2, f32[1,16,128]{2,1,0:T(8,128)} %bitcast.6), kind=kLoop, calls=%fused_computation.2 | loop fusion | flops 4096 | bytes 32768 | tf_op jit(solution)/shard_map/concatenate | solution.py:188
  36.4 4.0 %collective-permute-start.3 = (f32[2,16,128]{2,1,0:T(8,128)S(1)}, f32[2,16,128]{2,1,0:T(8,128)S(1)}, u32[]{:S(2)}, u32[]{:S(2)}) collective-permute-start(f32[2,16,128]{2,1,0:T(8,128)S(1)} %pad_maximum_fusion.2), channel_id=1, source_target_pairs={{0,2},{1,3},{2,0},{3,1},{4,6},{5,7},{6,4},{7,5},{8,10},{9,11},{10,... | collective-permute-start | bytes 49160 | tf_op jit(solution)/shard_map/ppermute | solution.py:176
  40.4 1.7 %collective-permute-done.3 = f32[2,16,128]{2,1,0:T(8,128)S(1)} collective-permute-done((f32[2,16,128]{2,1,0:T(8,128)S(1)}, f32[2,16,128]{2,1,0:T(8,128)S(1)}, u32[]{:S(2)}, u32[]{:S(2)}) %collective-permute-start.3) | collective-permute-done | bytes 16416 | tf_op jit(solution)/shard_map/ppermute | solution.py:176
  42.1 0.7 %pad_maximum_fusion.1 = f32[4,16,128]{2,1,0:T(8,128)S(1)} fusion(f32[2,16,128]{2,1,0:T(8,128)S(1)} %collective-permute-done.3, f32[1,16,128]{2,1,0:T(8,128)S(1)} %collective-permute-done.2, f32[1,16,128]{2,1,0:T(8,128)} %bitcast.7), kind=kLoop, calls=%fused_computation.1 | loop fusion | flops 16384 | bytes 65536 | tf_op jit(solution)/shard_map/concatenate | solution.py:188
  42.8 0.0 collective-permute-start.4
  42.8 1.2 %collective-permute-done.4 = f32[4,16,128]{2,1,0:T(8,128)S(1)} collective-permute-done((f32[4,16,128]{2,1,0:T(8,128)S(1)}, f32[4,16,128]{2,1,0:T(8,128)S(1)}, u32[]{:S(2)}, u32[]{:S(2)}) %collective-permute-start.4) | collective-permute-done | bytes 32800 | tf_op jit(solution)/shard_map/ppermute | solution.py:176
  44.0 1.3 %pad_maximum_fusion.vectors = f32[8,16,128]{2,1,0:T(8,128)} fusion(f32[4,16,128]{2,1,0:T(8,128)S(1)} %collective-permute-done.4, f32[2,16,128]{2,1,0:T(8,128)S(1)} %collective-permute-done.3, f32[1,16,128]{2,1,0:T(8,128)S(1)} %collective-permute-done.2, f32[1,16,128]{2,1,0:T(8,128)} %bitcast.8), kind=kLoop, calls=%fused_computation | loop fusion | flops 49152 | bytes 131072 | tf_op jit(solution)/shard_map/concatenate | solution.py:189
  45.3 2.2 %gram.1 = (f32[2,512]{1,0:T(2,128)}, f32[512,512]{1,0:T(8,128)}) custom-call(s32[8]{0:T(128)} %assignment.1, f32[8,16,128]{2,1,0:T(8,128)} %pad_maximum_fusion.vectors), custom_call_target="tpu_custom_call" | custom-call | tf_op jit(solution)/shard_map/gram/pallas_call | solution.py:162
  (1 shorter events, 0.0 us)
Async XLA Ops:
  0.6 1.2 %copy-start = (bf16[2,7168,32]{1,2,0:T(8,128)(2,1)S(1)}, bf16[2,7168,32]{1,2,0:T(8,128)(2,1)}, u32[]{:S(2)}) copy-start(bf16[2,7168,32]{1,2,0:T(8,128)(2,1)} %param.8) | copy-start | bytes 2752516
  1.8 0.9 %copy-start.1 = (bf16[2,2048,32]{1,2,0:T(8,128)(2,1)S(1)}, bf16[2,2048,32]{1,2,0:T(8,128)(2,1)}, u32[]{:S(2)}) copy-start(bf16[2,2048,32]{1,2,0:T(8,128)(2,1)} %param.9) | copy-start | bytes 786436
  2.8 0.7 %copy-start.2 = (s32[2]{0:T(128)S(1)}, s32[2]{0:T(128)}, u32[]{:S(2)}) copy-start(s32[2]{0:T(128)} %counts.1) | copy-start | bytes 28
  16.1 1.6 %collective-permute-start = (f32[2,64,512]{2,1,0:T(8,128)S(1)}, f32[2,64,512]{2,1,0:T(8,128)S(1)}, u32[]{:S(2)}, u32[]{:S(2)}) collective-permute-start(f32[2,64,512]{2,1,0:T(8,128)S(1)} %get-tuple-element.5), channel_id=1, source_target_pairs={{0,4},{4,0},{8,12},{12,8},{1,5},{5,1},{9,13},{13,9},{2,6},{6,2},{1... | collective-permute-start | bytes 786440 | tf_op jit(solution)/shard_map/ppermute | solution.py:176
  17.8 9.6 %copy-start.3 = (f32[2,64,512]{2,1,0:T(8,128)}, f32[2,64,512]{2,1,0:T(8,128)S(1)}, u32[]{:S(2)}) copy-start(f32[2,64,512]{2,1,0:T(8,128)S(1)} %add.3.own) | copy-start | bytes 786436
  17.8 9.6 %collective-permute-start.1 = (f32[2,64,512]{2,1,0:T(8,128)S(1)}, f32[2,64,512]{2,1,0:T(8,128)S(1)}, u32[]{:S(2)}, u32[]{:S(2)}) collective-permute-start(f32[2,64,512]{2,1,0:T(8,128)S(1)} %add.3.own), channel_id=1, source_target_pairs={{0,8},{4,12},{8,0},{12,4},{1,9},{5,13},{9,1},{13,5},{2,10},{6,14},... | collective-permute-start | bytes 786440 | tf_op jit(solution)/shard_map/ppermute | solution.py:176
  27.4 0.7 %copy-start.4 = (f32[2,64,512]{2,1,0:T(8,128)}, f32[2,64,512]{2,1,0:T(8,128)S(1)}, u32[]{:S(2)}) copy-start(f32[2,64,512]{2,1,0:T(8,128)S(1)} %collective-permute-done.1.received) | copy-start | bytes 786436
  30.0 5.7 %collective-permute-start.2 = (f32[1,16,128]{2,1,0:T(8,128)}, f32[1,16,128]{2,1,0:T(8,128)S(1)}, u32[]{:S(2)}, u32[]{:S(2)}) collective-permute-start(f32[1,16,128]{2,1,0:T(8,128)} %bitcast.5), channel_id=1, source_target_pairs={{0,1},{1,0},{2,3},{3,2},{4,5},{5,4},{6,7},{7,6},{8,9},{9,8},{10,11... | collective-permute-start | bytes 24584 | tf_op jit(solution)/shard_map/ppermute | solution.py:176
  36.4 5.7 %collective-permute-start.3 = (f32[2,16,128]{2,1,0:T(8,128)S(1)}, f32[2,16,128]{2,1,0:T(8,128)S(1)}, u32[]{:S(2)}, u32[]{:S(2)}) collective-permute-start(f32[2,16,128]{2,1,0:T(8,128)S(1)} %pad_maximum_fusion.2), channel_id=1, source_target_pairs={{0,2},{1,3},{2,0},{3,1},{4,6},{5,7},{6,4},{7,5},{8,10},{9,11},{10,... | collective-permute-start | bytes 49160 | tf_op jit(solution)/shard_map/ppermute | solution.py:176
  42.8 1.2 %collective-permute-start.4 = (f32[4,16,128]{2,1,0:T(8,128)S(1)}, f32[4,16,128]{2,1,0:T(8,128)S(1)}, u32[]{:S(2)}, u32[]{:S(2)}) collective-permute-start(f32[4,16,128]{2,1,0:T(8,128)S(1)} %pad_maximum_fusion.1), channel_id=1, source_target_pairs={{0,4},{4,0},{8,12},{12,8},{1,5},{5,1},{9,13},{13,9},{2,6},{6,2},{1... | collective-permute-start | bytes 98312 | tf_op jit(solution)/shard_map/ppermute | solution.py:176

commit v2 on v1

--- a/solution.py
+++ b/solution.py
@@ -85,7 +85,8 @@
     width_x, width_g = ff // 4, d
     jobs = 2 * layers * (ff // width_x + d // width_g)
     anywhere = pl.BlockSpec(memory_space=pl.ANY)
-    out = jax.ShapeDtypeStruct((layers, 2 * rank, tokens), jnp.float32)
+    out = pltpu.VMEM((layers, 2 * rank, tokens), jnp.float32)
+    operands = (valid_counts, layer_inputs, output_grads, jnp.swapaxes(in_proj, 1, 2), jnp.swapaxes(out_proj, 1, 2))
     return pl.pallas_call(
         functools.partial(project_kernel, tokens // 4, width_x, width_g, 3),
         out_shape=(out, out),
@@ -101,7 +102,7 @@
         ],
         compiler_params=pltpu.CompilerParams(vmem_limit_bytes=48 * 2**20),
         name="project",
-    )(valid_counts, layer_inputs, output_grads, jnp.swapaxes(in_proj, 1, 2), jnp.swapaxes(out_proj, 1, 2))
+    )(*[pltpu.with_memory_space_constraint(a, pltpu.HBM) for a in operands])
 
 
 def product_kernel(scale, own, received, out, square):
@@ -130,18 +131,24 @@
         in_specs=[pl.BlockSpec(memory_space=pltpu.VMEM)] * 2,
         out_specs=pl.BlockSpec(memory_space=pltpu.VMEM),
         scratch_shapes=[pltpu.VMEM((layers, rank, rank), jnp.float32)],
+        compiler_params=pltpu.CompilerParams(vmem_limit_bytes=4 * 2**20),
         name="product",
     )(own, received)
 
 
-def gram_kernel(assignment, vectors, seq_grads, fisher):
-    total = vectors.shape[0]
+def gram_kernel(assignment, near, far, seq_grads, fisher):
+    total = 2 * near.shape[0]
     local = seq_grads.shape[0]
     tensor, dp = lax.axis_index("tensor"), lax.axis_index("dp")
     core = lax.rem(tensor, 2)
     row_lanes, col_lanes = fisher.shape[0] // 128, fisher.shape[1] // 128
-    rows = jnp.concatenate([vectors[:, dp * row_lanes + r, :] for r in range(row_lanes)], axis=1)
-    cols = jnp.concatenate([vectors[:, tensor * col_lanes + r, :] for r in range(col_lanes)], axis=1)
+
+    def block(index, lanes):
+        return jnp.concatenate(
+            [jnp.concatenate([v[:, index * lanes + r, :] for r in range(lanes)], axis=1) for v in (near, far)], axis=0
+        )
+
+    rows, cols = block(dp, row_lanes), block(tensor, col_lanes)
     rows_high, rows_low = pieces(rows)
     cols_high, cols_low = pieces(cols)
     fisher[...] = lax.dot_general(
@@ -158,17 +165,18 @@
         seq_grads[r : r + 1, :] = chosen
 
 
-def gram(vectors, assignment, local, row_width, col_width):
+def gram(near, far, assignment, local, row_width, col_width):
     return pl.pallas_call(
         gram_kernel,
         out_shape=(
             jax.ShapeDtypeStruct((local, col_width), jnp.float32),
             jax.ShapeDtypeStruct((row_width, col_width), jnp.float32),
         ),
-        in_specs=[pl.BlockSpec(memory_space=pltpu.SMEM), pl.BlockSpec(memory_space=pltpu.VMEM)],
+        in_specs=[pl.BlockSpec(memory_space=pltpu.SMEM)] + [pl.BlockSpec(memory_space=pltpu.VMEM)] * 2,
         out_specs=(pl.BlockSpec(memory_space=pltpu.VMEM),) * 2,
+        compiler_params=pltpu.CompilerParams(vmem_limit_bytes=8 * 2**20),
         name="gram",
-    )(assignment, vectors)
+    )(pltpu.with_memory_space_constraint(assignment, pltpu.HBM), near, far)
 
 
 def swap(value, axis, bit):
@@ -186,8 +194,7 @@
     gathered = vector[None]
     for bit in (1, 2):
         gathered = jnp.concatenate([gathered, swap(gathered, "dp", bit)], axis=0)
-    gathered = jnp.concatenate([gathered, swap(gathered, "tensor", 1)], axis=0)
-    return gram(gathered, assignment, local, feat // lax.axis_size("dp"), feat // lax.axis_size("tensor"))
+    return gram(gathered, swap(gathered, "tensor", 1), assignment, local, feat // lax.axis_size("dp"), feat // lax.axis_size("tensor"))
 
 
 def any_sizes(layer_inputs, output_grads, in_proj, out_proj, valid_counts, assignment):

time: 46.8 us -> 38.8 us (0.83); the launches traced: 47.5 us -> 38 us
  local copies, waits for them, and re-layouts: 3.49 us -> 0 us
  other arithmetic: 2.76 us -> 0.05 us
  starting transfers between devices: 11.3 us -> 9.02 us
  Pallas kernels: 16.8 us -> 15.2 us
  waiting for transfers between devices: 12.5 us -> 13.1 us
    unnamed x10 -> x0, local copies, waits for them, and re-layouts: 3.49 us -> none
    ppermute x5, starting transfers between devices: 11.3 us -> 9.02 us  [swap(): return lax.ppermute(value, axis, [(i, i ^ bit) for i in range(size)])]
    pallas_call x1, Pallas kernels: 1.9 us -> 0.27 us  [product(): pl.pallas_call(functools.partial(product_kernel, tokens ** (-0.5)), out_s...]
    concatenate x2, other arithmetic: 1.4 us -> 0.01 us  [two_level(): gathered = jnp.concatenate([gathered, swap(gathered, 'dp', bit)], axis=0)]
    concatenate x1 -> x0, other arithmetic: 1.33 us -> none  [two_level(): gathered = jnp.concatenate([gathered, swap(gathered, 'tensor', 1)], axis=0)]
    ppermute x5, waiting for transfers between devices: 12.5 us -> 13.1 us  [swap(): return lax.ppermute(value, axis, [(i, i ^ bit) for i in range(size)])]
where the time goes in v2:
time: 38.8 us; the launch traced here: 38 us
  Pallas kernels  15.2 us (39%)
  waiting for transfers between devices  13.1 us (34%)
  starting transfers between devices  9.02 us (23%)
  between operations  0.65 us (2%)
    ppermute x5, waiting for transfers between devices, swap(): return lax.ppermute(value, axis, [(i, i ^ bit) for i in range(size)])  13.1 us
    pallas_call x1, Pallas kernels, project(): pl.pallas_call(functools.partial(project_kernel, tokens // 4, width_x, wi...  12.9 us
    ppermute x5, starting transfers between devices, swap(): return lax.ppermute(value, axis, [(i, i ^ bit) for i in range(size)])  9.02 us
    pallas_call x1, Pallas kernels, gram(): pl.pallas_call(gram_kernel, out_shape=(jax.ShapeDtypeStruct((local, col_w...  1.96 us
  transfers between devices with their start and end apart: 5, of which 5 were waited for; matrix products, arithmetic and copies ran while one was open for 0% of the time, Pallas kernels for 0%

profile of v2, /device:TPU:0, one launch (start us, length us, event | category | flops | bytes accessed | tf_op | source)
XLA Modules:
  0.0 38.0 jit_solution(17032831992711905120)
XLA Ops:
  0.6 12.9 %project.1 = (f32[2,64,512]{2,1,0:T(8,128)S(1)}, f32[2,64,512]{2,1,0:T(8,128)S(1)}) custom-call(s32[2]{0:T(128)} %counts.1, bf16[2,2,512,7168]{3,2,1,0:T(8,128)(2,1)} %x.1, bf16[2,2,512,2048]{3,2,1,0:T(8,128)(2,1)} %g.1, bf16[2,32,7168]{2,1,0:T(8,128)(2,1)} %bitcast.6, bf16[2,32,2048]{2,1,0:T(8,128)(2,1)} %bitcast.7), custom_call_target="tpu_custom_call" | custom-call | tf_op jit(solution)/shard_map/project/pallas_call | solution.py:90
  13.6 0.4 %collective-permute-start = (f32[2,64,512]{2,1,0:T(8,128)S(1)}, f32[2,64,512]{2,1,0:T(8,128)S(1)}, u32[]{:S(2)}, u32[]{:S(2)}) collective-permute-start(f32[2,64,512]{2,1,0:T(8,128)S(1)} %get-tuple-element.5), channel_id=1, source_target_pairs={{0,4},{4,0},{8,12},{12,8},{1,5},{5,1},{9,13},{13,9},{2,6},{6,2},{1... | collective-permute-start | bytes 786440 | tf_op jit(solution)/shard_map/ppermute | solution.py:184
  14.0 1.2 %collective-permute-done = f32[2,64,512]{2,1,0:T(8,128)S(1)} collective-permute-done((f32[2,64,512]{2,1,0:T(8,128)S(1)}, f32[2,64,512]{2,1,0:T(8,128)S(1)}, u32[]{:S(2)}, u32[]{:S(2)}) %collective-permute-start) | collective-permute-done | bytes 262176 | tf_op jit(solution)/shard_map/ppermute | solution.py:184
  15.2 3.0 %collective-permute-start.1 = (f32[2,64,512]{2,1,0:T(8,128)S(1)}, f32[2,64,512]{2,1,0:T(8,128)S(1)}, u32[]{:S(2)}, u32[]{:S(2)}) collective-permute-start(f32[2,64,512]{2,1,0:T(8,128)S(1)} %add.3.own), channel_id=1, source_target_pairs={{0,8},{4,12},{8,0},{12,4},{1,9},{5,13},{9,1},{13,5},{2,10},{6,14},... | collective-permute-start | bytes 786440 | tf_op jit(solution)/shard_map/ppermute | solution.py:184
  18.3 6.6 %collective-permute-done.1.received = f32[2,64,512]{2,1,0:T(8,128)S(1)} collective-permute-done((f32[2,64,512]{2,1,0:T(8,128)S(1)}, f32[2,64,512]{2,1,0:T(8,128)S(1)}, u32[]{:S(2)}, u32[]{:S(2)}) %collective-permute-start.1) | collective-permute-done | bytes 262176 | tf_op jit(solution)/shard_map/ppermute | solution.py:184
  24.9 0.3 product.1
  25.1 1.2 %collective-permute-start.2 = (f32[1,16,128]{2,1,0:T(8,128)S(1)}, f32[1,16,128]{2,1,0:T(8,128)S(1)}, u32[]{:S(2)}, u32[]{:S(2)}) collective-permute-start(f32[1,16,128]{2,1,0:T(8,128)S(1)} %bitcast.3), channel_id=1, source_target_pairs={{0,1},{1,0},{2,3},{3,2},{4,5},{5,4},{6,7},{7,6},{8,9},{9,8},{10,11... | collective-permute-start | bytes 24584 | tf_op jit(solution)/shard_map/ppermute | solution.py:184
  26.4 2.4 %collective-permute-done.2 = f32[1,16,128]{2,1,0:T(8,128)S(1)} collective-permute-done((f32[1,16,128]{2,1,0:T(8,128)S(1)}, f32[1,16,128]{2,1,0:T(8,128)S(1)}, u32[]{:S(2)}, u32[]{:S(2)}) %collective-permute-start.2) | collective-permute-done | bytes 8224 | tf_op jit(solution)/shard_map/ppermute | solution.py:184
  28.8 4.3 %collective-permute-start.3 = (f32[2,16,128]{2,1,0:T(8,128)S(1)}, f32[2,16,128]{2,1,0:T(8,128)S(1)}, u32[]{:S(2)}, u32[]{:S(2)}) collective-permute-start(f32[2,16,128]{2,1,0:T(8,128)S(1)} %pad_maximum_fusion.1), channel_id=1, source_target_pairs={{0,2},{1,3},{2,0},{3,1},{4,6},{5,7},{6,4},{7,5},{8,10},{9,11},{10,... | collective-permute-start | bytes 49160 | tf_op jit(solution)/shard_map/ppermute | solution.py:184
  33.1 1.7 %collective-permute-done.3 = f32[2,16,128]{2,1,0:T(8,128)S(1)} collective-permute-done((f32[2,16,128]{2,1,0:T(8,128)S(1)}, f32[2,16,128]{2,1,0:T(8,128)S(1)}, u32[]{:S(2)}, u32[]{:S(2)}) %collective-permute-start.3) | collective-permute-done | bytes 16416 | tf_op jit(solution)/shard_map/ppermute | solution.py:184
  34.8 0.0 collective-permute-start.4
  34.8 1.2 %collective-permute-done.4.far = f32[4,16,128]{2,1,0:T(8,128)S(1)} collective-permute-done((f32[4,16,128]{2,1,0:T(8,128)S(1)}, f32[4,16,128]{2,1,0:T(8,128)S(1)}, u32[]{:S(2)}, u32[]{:S(2)}) %collective-permute-start.4) | collective-permute-done | bytes 32800 | tf_op jit(solution)/shard_map/ppermute | solution.py:184
  36.1 2.0 %gram.1 = (f32[2,512]{1,0:T(2,128)}, f32[512,512]{1,0:T(8,128)}) custom-call(s32[8]{0:T(128)} %assignment.1, f32[4,16,128]{2,1,0:T(8,128)S(1)} %pad_maximum_fusion.near, f32[4,16,128]{2,1,0:T(8,128)S(1)} %collective-permute-done.4.far), custom_call_target="tpu_custom_call" | custom-call | tf_op jit(solution)/shard_map/gram/pallas_call | solution.py:169
  (3 shorter events, 0.1 us)
Async XLA Ops:
  13.6 1.6 %collective-permute-start = (f32[2,64,512]{2,1,0:T(8,128)S(1)}, f32[2,64,512]{2,1,0:T(8,128)S(1)}, u32[]{:S(2)}, u32[]{:S(2)}) collective-permute-start(f32[2,64,512]{2,1,0:T(8,128)S(1)} %get-tuple-element.5), channel_id=1, source_target_pairs={{0,4},{4,0},{8,12},{12,8},{1,5},{5,1},{9,13},{13,9},{2,6},{6,2},{1... | collective-permute-start | bytes 786440 | tf_op jit(solution)/shard_map/ppermute | solution.py:184
  15.2 9.6 %collective-permute-start.1 = (f32[2,64,512]{2,1,0:T(8,128)S(1)}, f32[2,64,512]{2,1,0:T(8,128)S(1)}, u32[]{:S(2)}, u32[]{:S(2)}) collective-permute-start(f32[2,64,512]{2,1,0:T(8,128)S(1)} %add.3.own), channel_id=1, source_target_pairs={{0,8},{4,12},{8,0},{12,4},{1,9},{5,13},{9,1},{13,5},{2,10},{6,14},... | collective-permute-start | bytes 786440 | tf_op jit(solution)/shard_map/ppermute | solution.py:184
  25.1 3.7 %collective-permute-start.2 = (f32[1,16,128]{2,1,0:T(8,128)S(1)}, f32[1,16,128]{2,1,0:T(8,128)S(1)}, u32[]{:S(2)}, u32[]{:S(2)}) collective-permute-start(f32[1,16,128]{2,1,0:T(8,128)S(1)} %bitcast.3), channel_id=1, source_target_pairs={{0,1},{1,0},{2,3},{3,2},{4,5},{5,4},{6,7},{7,6},{8,9},{9,8},{10,11... | collective-permute-start | bytes 24584 | tf_op jit(solution)/shard_map/ppermute | solution.py:184
  28.8 6.0 %collective-permute-start.3 = (f32[2,16,128]{2,1,0:T(8,128)S(1)}, f32[2,16,128]{2,1,0:T(8,128)S(1)}, u32[]{:S(2)}, u32[]{:S(2)}) collective-permute-start(f32[2,16,128]{2,1,0:T(8,128)S(1)} %pad_maximum_fusion.1), channel_id=1, source_target_pairs={{0,2},{1,3},{2,0},{3,1},{4,6},{5,7},{6,4},{7,5},{8,10},{9,11},{10,... | collective-permute-start | bytes 49160 | tf_op jit(solution)/shard_map/ppermute | solution.py:184
  34.8 1.2 %collective-permute-start.4 = (f32[4,16,128]{2,1,0:T(8,128)S(1)}, f32[4,16,128]{2,1,0:T(8,128)S(1)}, u32[]{:S(2)}, u32[]{:S(2)}) collective-permute-start(f32[4,16,128]{2,1,0:T(8,128)S(1)} %pad_maximum_fusion.near), channel_id=1, source_target_pairs={{0,4},{4,0},{8,12},{12,8},{1,5},{5,1},{9,13},{13,9},{2,6},{6,2},{1... | collective-permute-start | bytes 98312 | tf_op jit(solution)/shard_map/ppermute | solution.py:184
